TPU v7x, 32 devices: a whole 2x2x4 slice. The times are simulated.
32 devices in a mesh: gz: 8 (over z, y), col: 4 (over x, core).
Axes of the slice: x: 2, y: 2, z: 4, core: 2. Of those that a mesh axis runs over, the one named last changes fastest.
Arguments:
- volume: bfloat16 [32, 64, 32, 256], P(None, 'gz', 'col'), may hold values from -6 to 6
- cotangent: bfloat16 [64, 32, 16, 128], P(None, 'gz', 'col'), may hold values from -6 to 6
- weight: bfloat16 [64, 864], P('col'), may hold values from -0.21875 to 0.21875
- bias: bfloat16 [64], P('col'), may hold values from -1 to 1
Outputs:
- input_grad: bfloat16 [32, 64, 32, 256], P(None, 'gz', 'col')
- filter_grad: float32 [64, 864], P('col')
- bias_grad: float32 [64], P('col')
All inputs are finite; a program needn't handle non-finite values.
Results may differ from a plain program's by a relative error of at most 0.006.
Values may be sent and summed in bfloat16 or wider, within the bound.
A program may use at most 64 MiB of HBM per device.

v0:
```python
import math

import jax
import jax.numpy as jnp
from jax import lax
from jax.sharding import PartitionSpec as P

RIM_SETS = (((0, 0), (2, 1)), ((1, 0),))
CELL_SETS = ((1,), (2, 0))


def from_behind(block, axis, distance):
    devices = range(lax.axis_size(axis))
    route = [((i - distance) % len(devices), i) for i in devices]
    return lax.ppermute(block, axis, route)


def slope(value):
    sigmoid_value = jax.nn.sigmoid(value)
    return sigmoid_value * (1.0 + value * (1.0 - sigmoid_value))


def columns(extended, planes, rows):
    even_cells = extended[..., 0::2]
    odd_cells = extended[..., 1::2]
    chosen = (jnp.roll(odd_cells, 1, axis=-1), even_cells, odd_cells)
    stacked = []
    for depth in range(3):
        for height in range(3):
            for across in range(3):
                stacked.append(
                    chosen[across][
                        :, depth : depth + 2 * planes - 1 : 2, height : height + 2 * rows - 1 : 2, :
                    ]
                )
    stacked = jnp.stack(stacked)
    return stacked.reshape(-1, planes * rows * stacked.shape[-1])


def alternate(even, odd, axis):
    surplus = even.shape[axis] - odd.shape[axis]
    widths = [(0, 0)] * even.ndim
    widths[axis] = (0, surplus)
    odd = jnp.pad(odd, widths)
    merged = jnp.stack([even, odd], axis=axis + 1)
    shape = list(even.shape)
    shape[axis] = 2 * even.shape[axis]
    merged = merged.reshape(shape)
    return lax.slice_in_dim(merged, 0, 2 * even.shape[axis] - surplus, axis=axis)


def local(volume, cotangent, weight, bias):
    channels = volume.shape[0]
    outputs = cotangent.shape[0]
    planes = cotangent.shape[1]
    rows = cotangent.shape[2]
    wide = cotangent.shape[3]
    local_outputs = weight.shape[0]
    full_weight, full_bias = (
        lax.all_gather(weight, "col", axis=0, tiled=True),
        lax.all_gather(bias, "col", axis=0, tiled=True),
    )
    edge_plane = from_behind(volume[:, -1:], "gz", 1)
    padded = jnp.concatenate([edge_plane, volume], axis=1)
    edge_row = from_behind(padded[:, :, -1:], "col", 1)
    padded = jnp.concatenate([edge_row, padded], axis=2)
    gathered = columns(padded, planes, rows)
    preact = (
        jnp.dot(full_weight, gathered, preferred_element_type=jnp.float32)
        + full_bias.astype(jnp.float32)[:, None]
    )
    pre_grad = (cotangent.reshape(outputs, -1).astype(jnp.float32) * slope(preact)).astype(
        jnp.bfloat16
    )
    filter_part = lax.dot_general(
        pre_grad, gathered, (((1,), (1,)), ((), ())), preferred_element_type=jnp.float32
    )
    bias_part = jnp.sum(pre_grad.astype(jnp.float32), axis=1)
    total_filter, total_bias = lax.psum((filter_part, bias_part), ("gz", "col"))
    first_output = lax.axis_index("col") * local_outputs
    filter_sum = lax.dynamic_slice_in_dim(total_filter, first_output, local_outputs, 0)
    bias_sum = lax.dynamic_slice_in_dim(total_bias, first_output, local_outputs, 0)
    scale = 1.0 / math.sqrt(planes * rows * wide * lax.axis_size("gz") * lax.axis_size("col"))
    classes = {}
    for parity_z in range(2):
        for parity_y in range(2):
            for parity_x in range(2):
                plane_count = planes + 1 - parity_z
                row_count = rows + 1 - parity_y
                total = None
                for depth, shift_z in RIM_SETS[parity_z]:
                    for height, shift_y in RIM_SETS[parity_y]:
                        for across in CELL_SETS[parity_x]:
                            tap = 9 * depth + 3 * height + across
                            part = full_weight[:, tap * channels : (tap + 1) * channels]
                            piece = lax.dot_general(
                                part,
                                pre_grad,
                                (((0,), (0,)), ((), ())),
                                preferred_element_type=jnp.float32,
                            )
                            piece = piece.reshape(channels, planes, rows, wide)
                            if across == 0:
                                piece = jnp.roll(piece, -1, axis=-1)
                            piece = jnp.pad(
                                piece,
                                (
                                    (0, 0),
                                    (shift_z, plane_count - planes - shift_z),
                                    (shift_y, row_count - rows - shift_y),
                                    (0, 0),
                                ),
                            )
                            total = piece if total is None else total + piece
                classes[parity_z, parity_y, parity_x] = total
    by_rows = []
    for parity_z in range(2):
        by_cells = [
            alternate(classes[parity_z, parity_y, 0], classes[parity_z, parity_y, 1], 3)
            for parity_y in range(2)
        ]
        by_rows.append(alternate(by_cells[0], by_cells[1], 2))
    spread = alternate(by_rows[0], by_rows[1], 1)
    back_row = from_behind(spread[:, :, :1].astype(jnp.bfloat16), "col", -1).astype(jnp.float32)
    spread = spread[:, :, 1:]
    spread = spread.at[:, :, -1:].add(back_row)
    back_plane = from_behind(spread[:, :1].astype(jnp.bfloat16), "gz", -1).astype(jnp.float32)
    spread = spread[:, 1:]
    spread = spread.at[:, -1:].add(back_plane)
    input_grad = spread.astype(jnp.bfloat16)
    return (input_grad, filter_sum * scale, bias_sum * scale)


def solution(mesh):
    placed = (P(None, "gz", "col", None), P(None, "gz", "col", None), P("col", None), P("col"))
    return jax.shard_map(
        local,
        mesh=mesh,
        in_specs=placed,
        out_specs=(P(None, "gz", "col", None), P("col", None), P("col")),
        check_vma=False,
    )
```

profile of v0, /device:TPU:0, one launch (start us, length us, event | category | flops | bytes accessed | tf_op | source)
XLA Modules:
  0.0 320.0 jit_solution(4119833955320133626)
XLA Ops:
  8.2 3.0 collective-permute-start
  11.2 6.5 %collective-permute-done = bf16[32,1,8,256]{3,0,2,1:T(8,128)(2,1)S(1)} collective-permute-done((bf16[32,1,8,256]{3,0,2,1:T(8,128)(2,1)S(1)}, bf16[32,1,8,256]{3,0,2,1:T(8,128)(2,1)S(1)}, u32[]{:S(2)}, u32[]{:S(2)}) %collective-permute-start) | collective-permute-done | bytes 131104 | tf_op jit(solution)/shard_map/ppermute | solution.py:15
  17.7 1.8 constant_dynamic-update-slice_fusion
  22.4 7.3 %all-reduce.27 = bf16[64]{0:T(256)(128)(2,1)S(1)} all-reduce(bf16[64]{0:T(256)(128)(2,1)S(1)} %dynamic-update-slice.6), channel_id=1, replica_groups=mesh['gz'=8,'col'=4] {'col'}, use_global_device_ids=true, to_apply=%add.27 | all-reduce | flops 64 | bytes 256
  29.8 1.9 reshape.245
  31.6 5.8 %all_gather.6 = bf16[64,864]{1,0:T(8,128)(2,1)} all-gather(bf16[16,864]{1,0:T(8,128)(2,1)S(1)} %copy-done.12), channel_id=1, replica_groups=mesh['gz'=8,'col'=4] {'col'}, dimensions={0}, use_global_device_ids=true | all-gather | bytes 138240 | tf_op jit(solution)/shard_map/all_gather | solution.py:60
  37.6 27.9 %slice.323 = bf16[32,9,9,128]{3,0,2,1:T(8,128)(2,1)S(1)} slice(bf16[32,9,9,256]{3,0,2,1:T(8,128)(2,1)S(1)} %pad_maximum_fusion.2), slice={[0:32:1], [0:9:1], [0:9:1], [1:256:2]} | slice | bytes 1327104 | tf_op jit(solution)/shard_map/slice | solution.py:25
  65.5 27.9 %slice.327 = bf16[32,9,9,128]{3,0,2,1:T(8,128)(2,1)S(1)} slice(bf16[32,9,9,256]{3,0,2,1:T(8,128)(2,1)S(1)} %pad_maximum_fusion.2), slice={[0:32:1], [0:9:1], [0:9:1], [0:256:2]} | slice | bytes 1327104 | tf_op jit(solution)/shard_map/slice | solution.py:24
  94.8 1.8 copy.204
  96.6 4.2 %reshape.213 = bf16[864,2048]{1,0:T(8,128)(2,1)} reshape(bf16[27,32,4,4,128]{4,3,2,1,0:T(4,128)(2,1)S(1)} %copy.204) | data formatting | bytes 7077888 | tf_op jit(solution)/shard_map/reshape | solution.py:37
  100.8 3.1 convert_reduce_fusion
  134.6 1.8 reshape.218
  136.4 1.8 copy.209
  138.2 1.8 reshape.220
  140.0 1.7 copy.212
  141.8 1.8 reshape.222
  143.6 1.7 copy.215
  145.4 1.8 reshape.224
  148.6 1.5 fusion.2
  151.1 3.7 %copy.221 = f32[32,5,5,128,2]{0,4,3,2,1:T(2,128)S(1)} copy(f32[32,5,5,128,2]{3,0,2,1,4:T(8,128)} %pad_maximum_fusion.4) | data formatting | bytes 1638400 | tf_op jit(solution)/shard_map/stack | solution.py:45
  154.8 1.9 copy.232
  164.8 1.3 pad_maximum_fusion.1
  170.0 1.3 copy.241
  180.5 1.5 collective-permute-start.2
  182.1 1.9 fusion.46
  184.0 1.6 slice.458
  185.6 37.8 %psum.15 = f32[64]{0:T(128)S(1)} all-reduce(f32[64]{0:T(128)S(1)} %get-tuple-element.39), channel_id=1, replica_groups=mesh['gz'=8,'col'=4] {'gz','col'}, use_global_device_ids=true, to_apply=%region_2.3 | all-reduce | flops 64 | bytes 512 | tf_op jit(solution)/shard_map/psum | solution.py:79
  225.3 3.9 %collective-permute-start.3 = (bf16[32,1,8,256]{3,0,2,1:T(8,128)(2,1)S(1)}, bf16[32,1,8,256]{3,0,2,1:T(8,128)(2,1)S(1)}, u32[]{:S(2)}, u32[]{:S(2)}) collective-permute-start(bf16[32,1,8,256]{3,0,2,1:T(8,128)(2,1)S(1)} %slice.555), channel_id=1, source_target_pairs={{4,0},{8,4},{12,8},{16,12},{20,16},{24,20},{28,24},{0,28},{5,1},{9... | collective-permute-start | bytes 393224 | tf_op jit(solution)/shard_map/ppermute | solution.py:15
  229.7 77.7 %all-reduce.30.cloned.1.call-done = f32[64,864]{1,0:T(8,128)} async-done(((f32[64,864]{1,0:T(8,128)}), f32[64,864]{1,0:T(8,128)}) %all-reduce.30.cloned.1.call-update) | async-done | bytes 221200 | tf_op jit(solution)/shard_map/psum | solution.py:79
  307.4 1.4 dynamic-slice_multiply_fusion
  308.9 1.7 slice.461
  311.6 1.6 copy.251
  (187 shorter events, 61.5 us)
Async XLA Ops:
  7.2 24.5 %copy-start.12 = (bf16[16,864]{1,0:T(8,128)(2,1)S(1)}, bf16[16,864]{1,0:T(8,128)(2,1)}, u32[]{:S(2)}) copy-start(bf16[16,864]{1,0:T(8,128)(2,1)} %param.10) | copy-start | bytes 82948
  7.2 300.2 %all-reduce.30.cloned.1.call-start = ((), (), s32[]{:S(2)}) async-start(), calls=%async_computation | async-start | bytes 458752 | tf_op jit(solution)/shard_map/psum | solution.py:79
  8.2 9.6 %collective-permute-start = (bf16[32,1,8,256]{3,0,2,1:T(8,128)(2,1)S(1)}, bf16[32,1,8,256]{3,0,2,1:T(8,128)(2,1)S(1)}, u32[]{:S(2)}, u32[]{:S(2)}) collective-permute-start(bf16[32,1,8,256]{3,0,2,1:T(8,128)(2,1)S(1)} %copy.275), channel_id=1, source_target_pairs={{28,0},{0,4},{4,8},{8,12},{12,16},{16,20},{20,24},{24,28},{29,1},{... | collective-permute-start | bytes 393224 | tf_op jit(solution)/shard_map/ppermute | solution.py:15
  19.6 17.9 %collective-permute-start.1 = (bf16[32,9,1,256]{3,0,2,1:T(8,128)(2,1)S(1)}, bf16[32,9,1,256]{3,0,2,1:T(8,128)(2,1)S(1)}, u32[]{:S(2)}, u32[]{:S(2)}) collective-permute-start(bf16[32,9,1,256]{3,0,2,1:T(8,128)(2,1)S(1)} %slice.408), channel_id=1, source_target_pairs={{3,0},{0,1},{1,2},{2,3},{7,4},{4,5},{5,6},{6,7},{11,8},{8,9},{9,10... | collective-permute-start | bytes 442376 | tf_op jit(solution)/shard_map/ppermute | solution.py:15
  100.8 3.1 copy-start.2
  156.7 4.1 %copy-start.11 = (f32[32,2048]{1,0:T(8,128)S(1)}, f32[32,2048]{1,0:T(8,128)}, u32[]{:S(2)}) copy-start(f32[32,2048]{1,0:T(8,128)} %convolution_bitcast_fusion.13) | copy-start | bytes 786436
  156.7 4.4 %copy-start.10 = (f32[32,2048]{1,0:T(8,128)S(1)}, f32[32,2048]{1,0:T(8,128)}, u32[]{:S(2)}) copy-start(f32[32,2048]{1,0:T(8,128)} %convolution_bitcast_fusion.12) | copy-start | bytes 786436
  156.7 4.7 %copy-start.9 = (f32[32,2048]{1,0:T(8,128)S(1)}, f32[32,2048]{1,0:T(8,128)}, u32[]{:S(2)}) copy-start(f32[32,2048]{1,0:T(8,128)} %convolution_bitcast_fusion.10) | copy-start | bytes 786436
  164.7 2.7 copy-start.8
  164.8 3.1 copy-start.7
  166.1 2.2 copy-start.6
  166.2 2.5 copy-start.5
  166.2 2.8 copy-start.4
  167.4 1.8 copy-start.3
  178.4 1.4 copy-start.1
  180.1 2.0 copy-start
  180.5 43.0 %collective-permute-start.2 = (bf16[32,9,1,256]{3,0,2,1:T(8,128)(2,1)S(1)}, bf16[32,9,1,256]{3,0,2,1:T(8,128)(2,1)S(1)}, u32[]{:S(2)}, u32[]{:S(2)}) collective-permute-start(bf16[32,9,1,256]{3,0,2,1:T(8,128)(2,1)S(1)} %slice.554), channel_id=1, source_target_pairs={{1,0},{2,1},{3,2},{0,3},{5,4},{6,5},{7,6},{4,7},{9,8},{10,9},{11,1... | collective-permute-start | bytes 442376 | tf_op jit(solution)/shard_map/ppermute | solution.py:15
  225.3 85.3 %collective-permute-start.3 = (bf16[32,1,8,256]{3,0,2,1:T(8,128)(2,1)S(1)}, bf16[32,1,8,256]{3,0,2,1:T(8,128)(2,1)S(1)}, u32[]{:S(2)}, u32[]{:S(2)}) collective-permute-start(bf16[32,1,8,256]{3,0,2,1:T(8,128)(2,1)S(1)} %slice.555), channel_id=1, source_target_pairs={{4,0},{8,4},{12,8},{16,12},{20,16},{24,20},{28,24},{0,28},{5,1},{9... | collective-permute-start | bytes 393224 | tf_op jit(solution)/shard_map/ppermute | solution.py:15
Sparse Core Ops, SparseCore 0:
  185.8 121.6 all-reduce.29
where the time goes:
time: 322 us; the launch traced here: 320 us
  local copies, waits for them, and re-layouts  125 us (39%)
  waiting for transfers between devices  84.2 us (26%)
  blocking collectives  51 us (16%)
  matrix products  25.9 us (8%)
  between operations  15.6 us (5%)
  other arithmetic  9.32 us (3%)
  starting transfers between devices  8.49 us (3%)
    psum x1, waiting for transfers between devices, local(): total_filter, total_bias = lax.psum((filter_part, bias_part), ('gz', 'col'))  77.7 us
    psum x1, blocking collectives, local(): total_filter, total_bias = lax.psum((filter_part, bias_part), ('gz', 'col'))  37.8 us
    reshape x42, local copies, waits for them, and re-layouts, local(): piece = piece.reshape(channels, planes, rows, wide)  30.1 us
    slice x1, local copies, waits for them, and re-layouts, columns(): odd_cells = extended[..., 1::2]  27.9 us
    slice x1, local copies, waits for them, and re-layouts, columns(): even_cells = extended[..., 0::2]  27.9 us
    dot_general x27, matrix products, local(): lax.dot_general(part, pre_grad, (((0,), (0,)), ((), ())), preferred_eleme...  20.9 us
    another operation x13, local copies, waits for them, and re-layouts, alternate(): merged = jnp.stack([even, odd], axis=axis + 1)  13.5 us
    unnamed x78, local copies, waits for them, and re-layouts  8.75 us
  transfers between devices with their start and end apart: 5, of which 2 were waited for; matrix products, arithmetic and copies ran while one was open for 4% of the time, Pallas kernels for 0%

commit v1 on v0

v1 whole, which is shorter than its diff:
```python
import functools
import math

import jax
import jax.numpy as jnp
from jax import lax
from jax.experimental import pallas as pl
from jax.experimental.pallas import tpu as pltpu
from jax.sharding import PartitionSpec as P

MESH = pl.DeviceIdType.MESH
F32 = jnp.float32
BF16 = jnp.bfloat16
TAP_OF = {(0, 0): 1, (1, 0): 2, (1, 1): 0}
LANES = 128


def one_hot(shape, chosen):
    row = lax.broadcasted_iota(jnp.int32, shape, 0)
    column = lax.broadcasted_iota(jnp.int32, shape, 1)
    return jnp.where(chosen(row, column), 1.0, 0.0).astype(BF16)


def matmul(a, b):
    return jnp.dot(a, b, preferred_element_type=F32)


def kernel(
    n_gz, n_col, scale,
    vol, cot, weight,
    igrad, fgrad,
    cells, gathered, full, deltas, rolled, upstream, flat, back, stack,
    split, merge, to_rows, from_rows, swap,
    terms, slots, part, pieces, result,
    w_send, w_recv, v_send, v_recv, p_send, p_recv,
    r_send, r_recv, s_send, s_recv, g_send, g_recv,
):
    channels, planes_in, rows_in, wide_in = vol.shape
    planes, rows = planes_in // 2, rows_in // 2
    outputs = cot.shape[0]
    own = weight.shape[0]
    taps_wide = weight.shape[1]
    owners = taps_wide // LANES
    gz = lax.axis_index("gz")
    col = lax.axis_index("col")
    gz_next, gz_back = lax.rem(gz + 1, n_gz), lax.rem(gz + n_gz - 1, n_gz)
    col_next, col_back = lax.rem(col + 1, n_col), lax.rem(col + n_col - 1, n_col)

    barrier = pltpu.get_barrier_semaphore()
    for d in range(1, n_col):
        pl.semaphore_signal(
            barrier, inc=1, device_id=(gz, lax.rem(col + d, n_col)), device_id_type=MESH
        )

    def greet(d, carry):
        pl.semaphore_signal(
            barrier, inc=1, device_id=(lax.rem(gz + d, n_gz), col), device_id_type=MESH
        )
        return carry

    lax.fori_loop(1, n_gz, greet, 0)
    for there in ((gz_next, col_next), (gz_back, col_back)):
        pl.semaphore_signal(barrier, inc=1, device_id=there, device_id_type=MESH)

    side = wide_in
    split[...] = one_hot(
        (side, 3 * LANES),
        lambda r, c: r
        == jnp.where(
            c < LANES, 2 * c, jnp.where(c < 2 * LANES, 2 * (c - LANES) + 1, (2 * (c - 2 * LANES) + side - 1) % side)
        ),
    )
    merge[...] = one_hot((side, side), lambda r, c: c == 2 * (r % LANES) + r // LANES)
    area = channels * rows_in
    to_rows[...] = one_hot((area, area), lambda r, c: c == (r % channels) * rows_in + r // channels)
    from_rows[...] = one_hot((area, area), lambda r, c: c == (r % rows_in) * channels + r // rows_in)
    blocks = planes * rows
    group = swap.shape[0] // blocks
    swap[...] = one_hot(swap.shape, lambda r, c: c == (r % group) * blocks + r // group)

    def take_plane(p, carry):
        plane = vol[:, p].astype(F32).reshape(area, wide_in).astype(BF16)
        apart = matmul(plane, split[...]).astype(BF16)
        apart = matmul(to_rows[...], apart).astype(BF16)
        for y in range(rows_in):
            for t in range(3):
                cells[t, p + 1, y + 1] = apart[
                    y * channels : (y + 1) * channels, t * LANES : (t + 1) * LANES
                ]
        return carry

    take_plane(planes_in - 1, 0)
    pl.semaphore_wait(barrier, (n_col - 1) + (n_gz - 1) + 2)

    def send(src, dst, send_sem, recv_sem, there):
        return pltpu.make_async_remote_copy(
            src_ref=src, dst_ref=dst, send_sem=send_sem, recv_sem=recv_sem,
            device_id=there, device_id_type=MESH,
        )

    plane_copy = send(
        cells.at[0:2, planes_in, 1 : rows_in + 1], cells.at[0:2, 0, 1 : rows_in + 1],
        v_send.at[0], v_recv.at[0], (gz_next, col),
    )
    corner_copy = send(
        cells.at[0:2, planes_in, rows_in], cells.at[0:2, 0, 0],
        v_send.at[1], v_recv.at[1], (gz_next, col_next),
    )
    plane_copy.start()
    corner_copy.start()
    own_rows = pl.ds(pl.multiple_of(col * own, own), own)
    weight_copies = [
        send(
            weight, full.at[own_rows], w_send.at[d - 1], w_recv.at[d - 1],
            (gz, lax.rem(col + d, n_col)),
        )
        for d in range(1, n_col)
    ]
    for copy in weight_copies:
        copy.start()
    full[own_rows] = weight[...]
    lax.fori_loop(0, planes_in - 1, take_plane, 0)
    row_copy = send(
        cells.at[0:2, 1 : planes_in + 1, rows_in], cells.at[0:2, 1 : planes_in + 1, 0],
        v_send.at[2], v_recv.at[2], (gz, col_next),
    )
    row_copy.start()

    for g in range(outputs // group):
        piece = cot[g * group : (g + 1) * group].astype(F32).reshape(group * blocks, LANES)
        piece = matmul(swap[...], piece.astype(BF16))
        for b in range(blocks):
            upstream[b, g * group : (g + 1) * group] = piece[b * group : (b + 1) * group]
    first = 27 * channels
    spare = (taps_wide - first, gathered.shape[1])
    gathered[first:, :] = one_hot(spare, lambda r, c: r == 0)

    for copy in weight_copies:
        copy.wait()
    turned = full[...].astype(F32).T
    empty = jnp.zeros((channels, outputs), F32)
    for pz in range(2):
        for py in range(2):
            for px in range(2):
                kind = 4 * pz + 2 * py + px
                for sz in range(2):
                    for sy in range(2):
                        pair = []
                        for sx in range(2):
                            joined = ((pz, sz), (py, sy), (px, sx))
                            if all(j in TAP_OF for j in joined):
                                dz, dy, dx = (TAP_OF[j] for j in joined)
                                tap = 9 * dz + 3 * dy + dx
                                pair.append(turned[tap * channels : (tap + 1) * channels])
                            else:
                                pair.append(empty)
                        start = 2 * outputs * (2 * sz + sy)
                        back[
                            kind * channels : (kind + 1) * channels, start : start + 2 * outputs
                        ] = jnp.concatenate(pair, axis=1).astype(BF16)

    plane_copy.wait()
    corner_copy.wait()
    row_copy.wait()

    def turn(x, shift):
        return pltpu.roll(x.astype(F32), shift, 1).astype(BF16)

    for y in range(rows_in + 1):
        cells[2, 0, y] = turn(cells[1, 0, y], 1)
    for p in range(1, planes_in + 1):
        cells[2, p, 0] = turn(cells[1, p, 0], 1)

    def forward(k, carry):
        width = rows * LANES
        lanes = pl.ds(pl.multiple_of(k * width, width), width)
        for dz in range(3):
            for dy in range(3):
                for dx, t in enumerate((2, 0, 1)):
                    tap = 9 * dz + 3 * dy + dx
                    for j in range(rows):
                        place = pl.ds(pl.multiple_of(k * width + j * LANES, LANES), LANES)
                        gathered[tap * channels : (tap + 1) * channels, place] = cells[
                            t, 2 * k + dz, 2 * j + dy
                        ]
        preact = matmul(full[...], gathered[:, lanes])
        for j in range(rows):
            value = preact[:, j * LANES : (j + 1) * LANES]
            s = jax.nn.sigmoid(value)
            delta = upstream[k * rows + j] * (s * (1.0 + value * (1.0 - s)))
            delta = delta.astype(BF16)
            place = pl.ds(pl.multiple_of(k * width + j * LANES, LANES), LANES)
            flat[:, place] = delta
            deltas[k, j] = delta
            rolled[k, j] = turn(delta, LANES - 1)
        return carry

    lax.fori_loop(0, planes, forward, 0)
    halo_copies = [
        send(
            deltas.at[0, 0:rows], deltas.at[planes, 0:rows],
            p_send.at[0], p_recv.at[0], (gz_back, col),
        ),
        send(
            deltas.at[0, 0], deltas.at[planes, rows],
            p_send.at[1], p_recv.at[1], (gz_back, col_back),
        ),
        send(
            deltas.at[0:planes, 0], deltas.at[0:planes, rows],
            p_send.at[2], p_recv.at[2], (gz, col_back),
        ),
    ]
    for copy in halo_copies:
        copy.start()

    sums = lax.dot_general(
        flat[...], gathered[...], (((1,), (1,)), ((), ())), preferred_element_type=F32
    )
    for c in range(n_col):
        for i in range(owners):
            terms[c, i] = sums[c * own : (c + 1) * own, i * LANES : (i + 1) * LANES]
    term_copies = []
    for d in range(1, n_col):
        there = lax.rem(col + d, n_col)
        term_copies.append(
            send(terms.at[there], slots.at[d - 1], r_send.at[d - 1], r_recv.at[d - 1], (gz, there))
        )
    for copy in term_copies:
        copy.start()

    for copy in halo_copies:
        copy.wait()
    for j in range(rows + 1):
        rolled[planes, j] = turn(deltas[planes, j], LANES - 1)
    for k in range(planes):
        rolled[k, rows] = turn(deltas[k, rows], LANES - 1)

    def backward(k, carry):
        for sz in range(2):
            for sy in range(2):
                for sx, source in enumerate((deltas, rolled)):
                    start = outputs * (4 * sz + 2 * sy + sx)
                    for j in range(rows):
                        stack[start : start + outputs, j * LANES : (j + 1) * LANES] = source[
                            k + sz, j + sy
                        ]
        found = matmul(back[...], stack[...]).astype(BF16)
        for pz in range(2):
            tall = []
            for y in range(rows_in):
                j, py = y // 2, y % 2
                kind = 4 * pz + 2 * py
                tall.append(
                    jnp.concatenate(
                        [
                            found[
                                (kind + px) * channels : (kind + px + 1) * channels,
                                j * LANES : (j + 1) * LANES,
                            ]
                            for px in range(2)
                        ],
                        axis=1,
                    )
                )
            tall = jnp.concatenate(tall, axis=0)
            tall = matmul(tall, merge[...]).astype(BF16)
            tall = matmul(from_rows[...], tall)
            igrad[:, 2 * k + pz] = tall.reshape(channels, rows_in, wide_in).astype(BF16)
        return carry

    half = planes // 2
    lax.fori_loop(0, half, backward, 0)

    for copy in term_copies:
        copy.wait()
    total = terms[col]
    for d in range(1, n_col):
        total = total + slots[d - 1]
    part[...] = total

    def piece_copy(d):
        there = lax.rem(gz + d, n_gz)
        safe = lax.rem(there, owners)
        return there, send(
            part.at[safe], pieces.at[d - 1], s_send.at[d - 1], s_recv.at[d - 1], (there, col)
        )

    def piece_start(d, carry):
        there, copy = piece_copy(d)

        @pl.when(there < owners)
        def _():
            copy.start()

        return carry

    lax.fori_loop(1, n_gz, piece_start, 0)
    lax.fori_loop(half, planes - 1, backward, 0)

    def piece_sent(d, carry):
        there, copy = piece_copy(d)

        @pl.when(there < owners)
        def _():
            copy.wait_send()

        return carry

    lax.fori_loop(1, n_gz, piece_sent, 0)
    mine = lax.rem(gz, owners)

    def result_copy(d):
        return send(
            result.at[mine], result.at[mine], g_send.at[d - 1], g_recv.at[mine],
            (lax.rem(gz + d, n_gz), col),
        )

    @pl.when(gz < owners)
    def _():
        def collect(d, value):
            piece_copy(d)[1].wait_recv()
            return value + pieces[d - 1]

        result[mine] = lax.fori_loop(1, n_gz, collect, part[mine]) * scale

        def result_start(d, carry):
            result_copy(d).start()
            return carry

        lax.fori_loop(1, n_gz, result_start, 0)

    backward(planes - 1, 0)

    @pl.when(gz < owners)
    def _():
        def result_sent(d, carry):
            result_copy(d).wait_send()
            return carry

        lax.fori_loop(1, n_gz, result_sent, 0)

    for i in range(owners):

        @pl.when(gz != i)
        def _():
            send(
                result.at[i], result.at[i], g_send.at[0], g_recv.at[i], (gz_next, col)
            ).wait_recv()

    for i in range(owners):
        fgrad[:, i * LANES : (i + 1) * LANES] = result[i]


def local(n_gz, n_col, volume, cotangent, weight, bias):
    channels, planes_in, rows_in, wide_in = volume.shape
    outputs, planes, rows, wide = cotangent.shape
    own = weight.shape[0]
    taps_wide = -(-(weight.shape[1] + 1) // LANES) * LANES
    owners = taps_wide // LANES
    scale = 1.0 / math.sqrt(planes * rows * wide * n_gz * n_col)
    filters = jnp.concatenate(
        [
            weight,
            bias[:, None],
            jnp.zeros((own, taps_wide - weight.shape[1] - 1), weight.dtype),
        ],
        axis=1,
    )
    blocks = planes * rows
    area = channels * rows_in
    cells_out = blocks * wide
    vmem = pl.BlockSpec(memory_space=pltpu.VMEM)
    dma = pltpu.SemaphoreType.DMA
    input_grad, sums = pl.pallas_call(
        functools.partial(kernel, n_gz, n_col, scale),
        out_shape=(
            jax.ShapeDtypeStruct(volume.shape, BF16),
            jax.ShapeDtypeStruct((own, taps_wide), F32),
        ),
        in_specs=[vmem] * 3,
        out_specs=(vmem, vmem),
        scratch_shapes=[
            pltpu.VMEM((3, planes_in + 1, rows_in + 1, channels, LANES), BF16),
            pltpu.VMEM((taps_wide, cells_out), BF16),
            pltpu.VMEM((outputs, taps_wide), BF16),
            pltpu.VMEM((planes + 1, rows + 1, outputs, LANES), BF16),
            pltpu.VMEM((planes + 1, rows + 1, outputs, LANES), BF16),
            pltpu.VMEM((blocks, outputs, LANES), F32),
            pltpu.VMEM((outputs, cells_out), BF16),
            pltpu.VMEM((8 * channels, 8 * outputs), BF16),
            pltpu.VMEM((8 * outputs, rows * LANES), BF16),
            pltpu.VMEM((wide_in, 3 * LANES), BF16),
            pltpu.VMEM((wide_in, wide_in), BF16),
            pltpu.VMEM((area, area), BF16),
            pltpu.VMEM((area, area), BF16),
            pltpu.VMEM((16 * blocks, 16 * blocks), BF16),
            pltpu.VMEM((n_col, owners, own, LANES), F32),
            pltpu.VMEM((n_col - 1, owners, own, LANES), F32),
            pltpu.VMEM((owners, own, LANES), F32),
            pltpu.VMEM((n_gz - 1, own, LANES), F32),
            pltpu.VMEM((owners, own, LANES), F32),
            dma((n_col - 1,)), dma((n_col - 1,)),
            dma((3,)), dma((3,)),
            dma((3,)), dma((3,)),
            dma((n_col - 1,)), dma((n_col - 1,)),
            dma((n_gz - 1,)), dma((n_gz - 1,)),
            dma((n_gz - 1,)), dma((owners,)),
        ],
        compiler_params=pltpu.CompilerParams(
            collective_id=0, has_side_effects=True, vmem_limit_bytes=40 * 1024 * 1024
        ),
    )(volume, cotangent.reshape(outputs, blocks, wide), filters)
    width = weight.shape[1]
    return input_grad, sums[:, :width], sums[:, width]


def solution(mesh):
    placed = (P(None, "gz", "col", None), P(None, "gz", "col", None), P("col", None), P("col"))
    return jax.shard_map(
        functools.partial(local, mesh.shape["gz"], mesh.shape["col"]),
        mesh=mesh,
        in_specs=placed,
        out_specs=(P(None, "gz", "col", None), P("col", None), P("col")),
        check_vma=False,
    )
```

time: 322 us -> 35.3 us (0.11)
  local copies, waits for them, and re-layouts: 125 us -> 5.21 us
  waiting for transfers between devices: 84.2 us -> 0 us
  blocking collectives: 51 us -> 0 us
  Pallas kernels: 0 us -> 28.4 us
  matrix products: 25.9 us -> 0 us
  between operations: 15.6 us -> 0.66 us
  other arithmetic: 9.32 us -> 0.83 us
  starting transfers between devices: 8.49 us -> 0 us
    psum x1 -> x0, waiting for transfers between devices: 77.7 us -> none  [local(): total_filter, total_bias = lax.psum((filter_part, bias_part), ('gz', 'col'))]
    slice x19 -> x1, local copies, waits for them, and re-layouts: 63.2 us -> 0.69 us  [local(): return (input_grad, sums[:, :width], sums[:, width])]
    psum x1 -> x0, blocking collectives: 37.8 us -> none  [local(): total_filter, total_bias = lax.psum((filter_part, bias_part), ('gz', 'col'))]
    reshape x43 -> x0, local copies, waits for them, and re-layouts: 34.3 us -> none  [the longest x42 30.1 us: local(): piece = piece.reshape(channels, planes, rows, wide)]
    pallas_call x0 -> x1, Pallas kernels: none -> 28.4 us  [local(): pl.pallas_call(functools.partial(kernel, n_gz, n_col, scale), out_shape=(...]
    dot_general x29 -> x0, matrix products: 25.9 us -> none  [the longest x27 20.9 us: local(): lax.dot_general(part, pre_grad, (((0,), (0,)), ((), ())), preferred_eleme...]
    another operation x15 -> x0, local copies, waits for them, and re-layouts: 15.3 us -> none  [the longest x13 13.5 us: alternate(): merged = jnp.stack([even, odd], axis=axis + 1)]
    ppermute x4 -> x0, starting transfers between devices: 8.45 us -> none  [from_behind(): return lax.ppermute(block, axis, route)]
  transfers between devices with their start and end apart: 5 -> 0, of which waited for: 2 -> 0; matrix products, arithmetic and copies ran while one was open for 4% -> 0% of each run, Pallas kernels for 0% -> 0%
where the time goes in v1:
time: 35.3 us; the launch traced here: 35.1 us
  Pallas kernels  28.4 us (80%)
  local copies, waits for them, and re-layouts  5.21 us (15%)
  other arithmetic  0.83 us (2%)
  between operations  0.66 us (2%)
    pallas_call x1, Pallas kernels, local(): pl.pallas_call(functools.partial(kernel, n_gz, n_col, scale), out_shape=(...  28.4 us
    unnamed x8, local copies, waits for them, and re-layouts  4.34 us
    concatenate x1, other arithmetic, local(): jnp.concatenate([weight, bias[:, None], jnp.zeros((own, taps_wide - weigh...  0.83 us

profile of v1, /device:TPU:0, one launch (start us, length us, event | category | flops | bytes accessed | tf_op | source)
XLA Modules:
  0.0 35.1 jit_solution(12386092575504649257)
XLA Ops:
  0.6 0.0 copy-start.2
  0.7 0.1 pad.2.clone
  0.7 0.6 %copy-done.2 = bf16[16]{0:T(256)(128)(2,1)S(1)} copy-done((bf16[16]{0:T(256)(128)(2,1)S(1)}, bf16[16]{0:T(256)(128)(2,1)}, u32[]{:S(2)}) %copy-start.2) | copy-done | bytes 56
  1.3 0.1 copy.8
  1.4 0.8 %maximum_maximum_fusion.weight = bf16[16,896]{1,0:T(8,128)(2,1)S(1)} fusion(bf16[16,1]{1,0:T(8,128)(2,1)S(1)} %copy.8, bf16[16,864]{1,0:T(8,128)(2,1)} %param.6, bf16[896]{0:T(1024)(128)(2,1)S(1)} %pad.2.clone), kind=kLoop, calls=%fused_computation | loop fusion | flops 86016 | bytes 58144 | tf_op jit(solution)/shard_map/concatenate | solution.py:361
  2.2 0.0 copy-start
  2.2 1.2 %copy-done = bf16[32,8,8,256]{3,2,1,0:T(8,128)(2,1)S(1)} copy-done((bf16[32,8,8,256]{3,2,1,0:T(8,128)(2,1)S(1)}, bf16[32,8,8,256]{3,2,1,0:T(8,128)(2,1)}, u32[]{:S(2)}) %copy-start) | copy-done | bytes 1048600
  3.4 0.0 copy-start.1
  3.4 0.9 %copy-done.1 = bf16[64,4,4,128]{3,2,1,0:T(4,128)(2,1)S(1)} copy-done((bf16[64,4,4,128]{3,2,1,0:T(4,128)(2,1)S(1)}, bf16[64,4,4,128]{3,2,1,0:T(4,128)(2,1)}, u32[]{:S(2)}) %copy-start.1) | copy-done | bytes 262168
  4.4 28.4 %shard_map.67 = (bf16[32,8,8,256]{3,2,1,0:T(8,128)(2,1)S(1)}, f32[16,896]{1,0:T(8,128)S(1)}) custom-call(bf16[32,8,8,256]{3,2,1,0:T(8,128)(2,1)S(1)} %copy-done, bf16[64,16,128]{2,1,0:T(8,128)(2,1)S(1)} %bitcast.3, bf16[16,896]{1,0:T(8,128)(2,1)S(1)} %maximum_maximum_fusion.weight), custom_call_target="tpu_custom_call" | custom-call | tf_op jit(solution)/shard_map/pallas_call | solution.py:374
  32.8 0.7 %slice_reduce_fusion = f32[16]{0:T(128)} fusion(f32[16,896]{1,0:T(8,128)S(1)} %get-tuple-element.6), kind=kLoop, calls=%fused_computation.1 | loop fusion | bytes 128 | tf_op jit(solution)/shard_map/slice | solution.py:414
  33.5 1.0 %copy.11 = bf16[32,8,8,256]{3,2,1,0:T(8,128)(2,1)} copy(bf16[32,8,8,256]{3,2,1,0:T(8,128)(2,1)S(1)} %get-tuple-element.10) | data formatting | bytes 2097152
  34.5 0.6 %copy.12 = f32[16,864]{1,0:T(8,128)} copy(f32[16,864]{1,0:T(8,128)S(1)} %bitcast.4) | data formatting | bytes 110592
  (1 shorter events, 0.0 us)
Async XLA Ops:
  0.6 0.7 %copy-start.2 = (bf16[16]{0:T(256)(128)(2,1)S(1)}, bf16[16]{0:T(256)(128)(2,1)}, u32[]{:S(2)}) copy-start(bf16[16]{0:T(256)(128)(2,1)} %param.7) | copy-start | bytes 100
  2.2 1.2 %copy-start = (bf16[32,8,8,256]{3,2,1,0:T(8,128)(2,1)S(1)}, bf16[32,8,8,256]{3,2,1,0:T(8,128)(2,1)}, u32[]{:S(2)}) copy-start(bf16[32,8,8,256]{3,2,1,0:T(8,128)(2,1)} %vol.1) | copy-start | bytes 3145732
  3.4 0.9 %copy-start.1 = (bf16[64,4,4,128]{3,2,1,0:T(4,128)(2,1)S(1)}, bf16[64,4,4,128]{3,2,1,0:T(4,128)(2,1)}, u32[]{:S(2)}) copy-start(bf16[64,4,4,128]{3,2,1,0:T(4,128)(2,1)} %param.5) | copy-start | bytes 786436

commit v2 on v1

--- a/solution.py
+++ b/solution.py
@@ -21,31 +21,51 @@
     return jnp.where(chosen(row, column), 1.0, 0.0).astype(BF16)
 
 
+def around(size, body, value):
+    if size > 16:
+        return lax.fori_loop(1, size, body, value)
+    for d in range(1, size):
+        value = body(d, value)
+    return value
+
+
 def matmul(a, b):
     return jnp.dot(a, b, preferred_element_type=F32)
 
 
 def kernel(
     n_gz, n_col, scale,
-    vol, cot, weight,
-    igrad, fgrad,
+    volume, cotangent, weight_in, bias_in,
+    igrad, fgrad, bgrad,
+    vol, cot, weight_own, bias_own, weight,
     cells, gathered, full, deltas, rolled, upstream, flat, back, stack,
     split, merge, to_rows, from_rows, swap,
     terms, slots, part, pieces, result,
-    w_send, w_recv, v_send, v_recv, p_send, p_recv,
+    load, w_send, w_recv, v_send, v_recv, p_send, p_recv,
     r_send, r_recv, s_send, s_recv, g_send, g_recv,
 ):
     channels, planes_in, rows_in, wide_in = vol.shape
     planes, rows = planes_in // 2, rows_in // 2
     outputs = cot.shape[0]
-    own = weight.shape[0]
-    taps_wide = weight.shape[1]
+    own, taps_wide = weight.shape
     owners = taps_wide // LANES
     gz = lax.axis_index("gz")
     col = lax.axis_index("col")
     gz_next, gz_back = lax.rem(gz + 1, n_gz), lax.rem(gz + n_gz - 1, n_gz)
     col_next, col_back = lax.rem(col + 1, n_col), lax.rem(col + n_col - 1, n_col)
 
+    loads = [pltpu.make_async_copy(weight_in, weight_own, load.at[planes_in])]
+    loads.append(pltpu.make_async_copy(bias_in, bias_own, load.at[planes_in + 1]))
+    loads.append(pltpu.make_async_copy(cotangent, cot, load.at[planes_in + 2]))
+
+    def plane_load(p):
+        return pltpu.make_async_copy(volume.at[:, p], vol.at[:, p], load.at[p])
+
+    plane_load(planes_in - 1).start()
+    for copy in loads:
+        copy.start()
+    for p in range(planes_in - 1):
+        plane_load(p).start()
     barrier = pltpu.get_barrier_semaphore()
     for d in range(1, n_col):
         pl.semaphore_signal(
@@ -58,17 +78,13 @@
         )
         return carry
 
-    lax.fori_loop(1, n_gz, greet, 0)
+    around(n_gz, greet, 0)
     for there in ((gz_next, col_next), (gz_back, col_back)):
         pl.semaphore_signal(barrier, inc=1, device_id=there, device_id_type=MESH)
 
     side = wide_in
     split[...] = one_hot(
-        (side, 3 * LANES),
-        lambda r, c: r
-        == jnp.where(
-            c < LANES, 2 * c, jnp.where(c < 2 * LANES, 2 * (c - LANES) + 1, (2 * (c - 2 * LANES) + side - 1) % side)
-        ),
+        (side, side), lambda r, c: r == 2 * (c % LANES) + c // LANES
     )
     merge[...] = one_hot((side, side), lambda r, c: c == 2 * (r % LANES) + r // LANES)
     area = channels * rows_in
@@ -78,18 +94,36 @@
     group = swap.shape[0] // blocks
     swap[...] = one_hot(swap.shape, lambda r, c: c == (r % group) * blocks + r // group)
 
-    def take_plane(p, carry):
+    loads[0].wait()
+    loads[1].wait()
+    taps_own = weight_own.shape[1]
+    tail = taps_wide - LANES
+    square = (own, own)
+    diagonal = lax.broadcasted_iota(jnp.int32, square, 0) == lax.broadcasted_iota(
+        jnp.int32, square, 1
+    )
+    spread = jnp.broadcast_to(bias_own[...].astype(F32), square)
+    column = jnp.sum(jnp.where(diagonal, spread, 0.0), axis=1, keepdims=True)
+    spare_own = (own, taps_wide - taps_own)
+    column = jnp.where(lax.broadcasted_iota(jnp.int32, spare_own, 1) == 0, column, 0.0)
+    weight[:, :tail] = weight_own[:, :tail]
+    weight[:, tail:] = jnp.concatenate(
+        [weight_own[:, tail:].astype(F32), column], axis=1
+    ).astype(BF16)
+
+    def take_plane(p):
+        plane_load(p).wait()
         plane = vol[:, p].astype(F32).reshape(area, wide_in).astype(BF16)
-        apart = matmul(plane, split[...]).astype(BF16)
-        apart = matmul(to_rows[...], apart).astype(BF16)
-        for y in range(rows_in):
-            for t in range(3):
-                cells[t, p + 1, y + 1] = apart[
-                    y * channels : (y + 1) * channels, t * LANES : (t + 1) * LANES
-                ]
-        return carry
-
-    take_plane(planes_in - 1, 0)
+        plane = matmul(to_rows[...], plane).astype(BF16)
+        apart = matmul(plane, split[...])
+        parts = [apart[:, :LANES], apart[:, LANES:]]
+        parts.append(pltpu.roll(parts[1], 1, 1))
+        for t in range(3):
+            narrow = parts[t].astype(BF16)
+            for y in range(rows_in):
+                cells[t, p + 1, y + 1] = narrow[y * channels : (y + 1) * channels]
+
+    take_plane(planes_in - 1)
     pl.semaphore_wait(barrier, (n_col - 1) + (n_gz - 1) + 2)
 
     def send(src, dst, send_sem, recv_sem, there):
@@ -119,13 +153,15 @@
     for copy in weight_copies:
         copy.start()
     full[own_rows] = weight[...]
-    lax.fori_loop(0, planes_in - 1, take_plane, 0)
+    for p in range(planes_in - 1):
+        take_plane(p)
     row_copy = send(
         cells.at[0:2, 1 : planes_in + 1, rows_in], cells.at[0:2, 1 : planes_in + 1, 0],
         v_send.at[2], v_recv.at[2], (gz, col_next),
     )
     row_copy.start()
 
+    loads[2].wait()
     for g in range(outputs // group):
         piece = cot[g * group : (g + 1) * group].astype(F32).reshape(group * blocks, LANES)
         piece = matmul(swap[...], piece.astype(BF16))
@@ -159,43 +195,42 @@
                             kind * channels : (kind + 1) * channels, start : start + 2 * outputs
                         ] = jnp.concatenate(pair, axis=1).astype(BF16)
 
+    def turn(x, shift):
+        return pltpu.roll(x.astype(F32), shift, 1).astype(BF16)
+
+    def forward(some, start):
+        for place, (k, j) in enumerate(some):
+            lanes = slice(start + place * LANES, start + (place + 1) * LANES)
+            for dz in range(3):
+                for dy in range(3):
+                    for dx, t in enumerate((2, 0, 1)):
+                        tap = 9 * dz + 3 * dy + dx
+                        gathered[tap * channels : (tap + 1) * channels, lanes] = cells[
+                            t, 2 * k + dz, 2 * j + dy
+                        ]
+        stop = start + len(some) * LANES
+        preact = matmul(full[...], gathered[:, start:stop])
+        for place, (k, j) in enumerate(some):
+            value = preact[:, place * LANES : (place + 1) * LANES]
+            s = jax.nn.sigmoid(value)
+            delta = upstream[k * rows + j] * (s * (1.0 + value * (1.0 - s)))
+            narrow = delta.astype(BF16)
+            flat[:, start + place * LANES : start + (place + 1) * LANES] = narrow
+            deltas[k, j] = narrow
+            rolled[k, j] = turn(narrow, LANES - 1)
+        return stop
+
+    inside = [(k, j) for k in range(1, planes) for j in range(1, rows)]
+    border = [(0, j) for j in range(rows)] + [(k, 0) for k in range(1, planes)]
+    reached = forward(inside, 0)
     plane_copy.wait()
     corner_copy.wait()
     row_copy.wait()
-
-    def turn(x, shift):
-        return pltpu.roll(x.astype(F32), shift, 1).astype(BF16)
-
     for y in range(rows_in + 1):
         cells[2, 0, y] = turn(cells[1, 0, y], 1)
     for p in range(1, planes_in + 1):
         cells[2, p, 0] = turn(cells[1, p, 0], 1)
-
-    def forward(k, carry):
-        width = rows * LANES
-        lanes = pl.ds(pl.multiple_of(k * width, width), width)
-        for dz in range(3):
-            for dy in range(3):
-                for dx, t in enumerate((2, 0, 1)):
-                    tap = 9 * dz + 3 * dy + dx
-                    for j in range(rows):
-                        place = pl.ds(pl.multiple_of(k * width + j * LANES, LANES), LANES)
-                        gathered[tap * channels : (tap + 1) * channels, place] = cells[
-                            t, 2 * k + dz, 2 * j + dy
-                        ]
-        preact = matmul(full[...], gathered[:, lanes])
-        for j in range(rows):
-            value = preact[:, j * LANES : (j + 1) * LANES]
-            s = jax.nn.sigmoid(value)
-            delta = upstream[k * rows + j] * (s * (1.0 + value * (1.0 - s)))
-            delta = delta.astype(BF16)
-            place = pl.ds(pl.multiple_of(k * width + j * LANES, LANES), LANES)
-            flat[:, place] = delta
-            deltas[k, j] = delta
-            rolled[k, j] = turn(delta, LANES - 1)
-        return carry
-
-    lax.fori_loop(0, planes, forward, 0)
+    forward(border, reached)
     halo_copies = [
         send(
             deltas.at[0, 0:rows], deltas.at[planes, 0:rows],
@@ -235,16 +270,16 @@
     for k in range(planes):
         rolled[k, rows] = turn(deltas[k, rows], LANES - 1)
 
-    def backward(k, carry):
+    def backward(k):
         for sz in range(2):
             for sy in range(2):
                 for sx, source in enumerate((deltas, rolled)):
                     start = outputs * (4 * sz + 2 * sy + sx)
                     for j in range(rows):
-                        stack[start : start + outputs, j * LANES : (j + 1) * LANES] = source[
+                        stack[k % 2, start : start + outputs, j * LANES : (j + 1) * LANES] = source[
                             k + sz, j + sy
                         ]
-        found = matmul(back[...], stack[...]).astype(BF16)
+        found = matmul(back[...], stack[k % 2]).astype(BF16)
         for pz in range(2):
             tall = []
             for y in range(rows_in):
@@ -266,10 +301,8 @@
             tall = matmul(tall, merge[...]).astype(BF16)
             tall = matmul(from_rows[...], tall)
             igrad[:, 2 * k + pz] = tall.reshape(channels, rows_in, wide_in).astype(BF16)
-        return carry
-
-    half = planes // 2
-    lax.fori_loop(0, half, backward, 0)
+
+    backward(0)
 
     for copy in term_copies:
         copy.wait()
@@ -294,8 +327,9 @@
 
         return carry
 
-    lax.fori_loop(1, n_gz, piece_start, 0)
-    lax.fori_loop(half, planes - 1, backward, 0)
+    around(n_gz, piece_start, 0)
+    for k in range(1, planes - 1):
+        backward(k)
 
     def piece_sent(d, carry):
         there, copy = piece_copy(d)
@@ -306,7 +340,7 @@
 
         return carry
 
-    lax.fori_loop(1, n_gz, piece_sent, 0)
+    around(n_gz, piece_sent, 0)
     mine = lax.rem(gz, owners)
 
     def result_copy(d):
@@ -321,15 +355,15 @@
             piece_copy(d)[1].wait_recv()
             return value + pieces[d - 1]
 
-        result[mine] = lax.fori_loop(1, n_gz, collect, part[mine]) * scale
+        result[mine] = around(n_gz, collect, part[mine]) * scale
 
         def result_start(d, carry):
             result_copy(d).start()
             return carry
 
-        lax.fori_loop(1, n_gz, result_start, 0)
-
-    backward(planes - 1, 0)
+        around(n_gz, result_start, 0)
+
+    backward(planes - 1)
 
     @pl.when(gz < owners)
     def _():
@@ -337,7 +371,7 @@
             result_copy(d).wait_send()
             return carry
 
-        lax.fori_loop(1, n_gz, result_sent, 0)
+        around(n_gz, result_sent, 0)
 
     for i in range(owners):
 
@@ -347,8 +381,12 @@
                 result.at[i], result.at[i], g_send.at[0], g_recv.at[i], (gz_next, col)
             ).wait_recv()
 
-    for i in range(owners):
+    for i in range(owners - 1):
         fgrad[:, i * LANES : (i + 1) * LANES] = result[i]
+    last = result[owners - 1]
+    fgrad[:, tail:] = last[:, : taps_own - tail]
+    column = jnp.broadcast_to(last[:, taps_own - tail : taps_own - tail + 1], square)
+    bgrad[...] = jnp.sum(jnp.where(diagonal, column, 0.0), axis=0, keepdims=True)
 
 
 def local(n_gz, n_col, volume, cotangent, weight, bias):
@@ -358,28 +396,27 @@
     taps_wide = -(-(weight.shape[1] + 1) // LANES) * LANES
     owners = taps_wide // LANES
     scale = 1.0 / math.sqrt(planes * rows * wide * n_gz * n_col)
-    filters = jnp.concatenate(
-        [
-            weight,
-            bias[:, None],
-            jnp.zeros((own, taps_wide - weight.shape[1] - 1), weight.dtype),
-        ],
-        axis=1,
-    )
     blocks = planes * rows
     area = channels * rows_in
     cells_out = blocks * wide
     vmem = pl.BlockSpec(memory_space=pltpu.VMEM)
+    hbm = pl.BlockSpec(memory_space=pltpu.HBM)
     dma = pltpu.SemaphoreType.DMA
-    input_grad, sums = pl.pallas_call(
+    input_grad, filter_grad, bias_grad = pl.pallas_call(
         functools.partial(kernel, n_gz, n_col, scale),
         out_shape=(
             jax.ShapeDtypeStruct(volume.shape, BF16),
-            jax.ShapeDtypeStruct((own, taps_wide), F32),
+            jax.ShapeDtypeStruct(weight.shape, F32),
+            jax.ShapeDtypeStruct((1, own), F32),
         ),
-        in_specs=[vmem] * 3,
-        out_specs=(vmem, vmem),
+        in_specs=[hbm] * 4,
+        out_specs=(vmem,) * 3,
         scratch_shapes=[
+            pltpu.VMEM(volume.shape, BF16),
+            pltpu.VMEM((outputs, blocks, wide), BF16),
+            pltpu.VMEM(weight.shape, BF16),
+            pltpu.VMEM((1, own), BF16),
+            pltpu.VMEM((own, taps_wide), BF16),
             pltpu.VMEM((3, planes_in + 1, rows_in + 1, channels, LANES), BF16),
             pltpu.VMEM((taps_wide, cells_out), BF16),
             pltpu.VMEM((outputs, taps_wide), BF16),
@@ -388,8 +425,8 @@
             pltpu.VMEM((blocks, outputs, LANES), F32),
             pltpu.VMEM((outputs, cells_out), BF16),
             pltpu.VMEM((8 * channels, 8 * outputs), BF16),
-            pltpu.VMEM((8 * outputs, rows * LANES), BF16),
-            pltpu.VMEM((wide_in, 3 * LANES), BF16),
+            pltpu.VMEM((2, 8 * outputs, rows * LANES), BF16),
+            pltpu.VMEM((wide_in, wide_in), BF16),
             pltpu.VMEM((wide_in, wide_in), BF16),
             pltpu.VMEM((area, area), BF16),
             pltpu.VMEM((area, area), BF16),
@@ -399,6 +436,7 @@
             pltpu.VMEM((owners, own, LANES), F32),
             pltpu.VMEM((n_gz - 1, own, LANES), F32),
             pltpu.VMEM((owners, own, LANES), F32),
+            dma((planes_in + 3,)),
             dma((n_col - 1,)), dma((n_col - 1,)),
             dma((3,)), dma((3,)),
             dma((3,)), dma((3,)),
@@ -407,11 +445,10 @@
             dma((n_gz - 1,)), dma((owners,)),
         ],
         compiler_params=pltpu.CompilerParams(
-            collective_id=0, has_side_effects=True, vmem_limit_bytes=40 * 1024 * 1024
+            collective_id=0, has_side_effects=True, vmem_limit_bytes=60 * 1024 * 1024
         ),
-    )(volume, cotangent.reshape(outputs, blocks, wide), filters)
-    width = weight.shape[1]
-    return input_grad, sums[:, :width], sums[:, width]
+    )(volume, cotangent.reshape(outputs, blocks, wide), weight, bias[None, :])
+    return input_grad, filter_grad, bias_grad.reshape(own)
 
 
 def solution(mesh):

time: 35.3 us -> 31.7 us (0.90)
  local copies, waits for them, and re-layouts: 5.21 us -> 3.46 us
  Pallas kernels: 28.4 us -> 27.4 us
  other arithmetic: 0.83 us -> 0 us
    pallas_call x1, Pallas kernels: 28.4 us -> 27.4 us  [local(): pl.pallas_call(functools.partial(kernel, n_gz, n_col, scale), out_shape=(...]
    unnamed x8 -> x7, local copies, waits for them, and re-layouts: 4.34 us -> 3.46 us
    concatenate x1 -> x0, other arithmetic: 0.83 us -> none  [local(): jnp.concatenate([weight, bias[:, None], jnp.zeros((own, taps_wide - weigh...]
    slice x1 -> x0, local copies, waits for them, and re-layouts: 0.69 us -> none  [local(): return (input_grad, sums[:, :width], sums[:, width])]
where the time goes in v2:
time: 31.7 us; the launch traced here: 31.5 us
  Pallas kernels  27.4 us (86%)
  local copies, waits for them, and re-layouts  3.46 us (11%)
  between operations  0.65 us (2%)
    pallas_call x1, Pallas kernels, local(): pl.pallas_call(functools.partial(kernel, n_gz, n_col, scale), out_shape=(...  27.4 us
    unnamed x7, local copies, waits for them, and re-layouts  3.46 us

profile of v2, /device:TPU:0, one launch (start us, length us, event | category | flops | bytes accessed | tf_op | source)
XLA Modules:
  0.0 31.5 jit_solution(4598229542306212523)
XLA Ops:
  0.6 27.4 %shard_map.67 = (bf16[32,8,8,256]{3,2,1,0:T(8,128)(2,1)}, f32[16,864]{1,0:T(8,128)}, f32[1,16]{1,0:T(1,128)}) custom-call(bf16[32,8,8,256]{3,2,1,0:T(8,128)(2,1)} %volume.1, bf16[64,16,128]{2,1,0:T(8,128)(2,1)} %bitcast.3, bf16[16,864]{1,0:T(8,128)(2,1)} %weight_in.1, bf16[1,16]{1,0:T(2,128)(2,1)} %bitcast.4), custom_call_target="tpu_custom_call" | custom-call | tf_op jit(solution)/shard_map/pallas_call | solution.py:405
  28.1 0.0 copy-start
  28.1 2.3 %copy.10 = bf16[32,8,8,256]{3,2,1,0:T(8,128)(2,1)} copy(bf16[32,8,8,256]{3,2,1,0:T(8,128)(2,1)} %get-tuple-element.12) | data formatting | bytes 2097152
  30.4 0.0 copy-done
  30.4 0.0 copy-start.1
  30.4 0.6 %copy.11 = f32[16,864]{1,0:T(8,128)} copy(f32[16,864]{1,0:T(8,128)S(1)} %copy-done) | data formatting | bytes 110592
  31.0 0.0 copy-done.1
  31.0 0.5 %copy.12 = f32[16]{0:T(128)} copy(f32[16]{0:T(128)S(1)} %bitcast.5) | data formatting | bytes 128
Async XLA Ops:
  28.1 2.3 %copy-start = (f32[16,864]{1,0:T(8,128)S(1)}, f32[16,864]{1,0:T(8,128)}, u32[]{:S(2)}) copy-start(f32[16,864]{1,0:T(8,128)} %get-tuple-element.13) | copy-start | bytes 165892
  30.4 0.6 %copy-start.1 = (f32[1,16]{1,0:T(1,128)S(1)}, f32[1,16]{1,0:T(1,128)}, u32[]{:S(2)}) copy-start(f32[1,16]{1,0:T(1,128)} %get-tuple-element.8) | copy-start | bytes 196

commit v3 on v2

--- a/solution.py
+++ b/solution.py
@@ -38,7 +38,7 @@
     volume, cotangent, weight_in, bias_in,
     igrad, fgrad, bgrad,
     vol, cot, weight_own, bias_own, weight,
-    cells, gathered, full, deltas, rolled, upstream, flat, back, stack,
+    edge, cells, gathered, full, deltas, rolled, upstream, flat, back, stack,
     split, merge, to_rows, from_rows, swap,
     terms, slots, part, pieces, result,
     load, w_send, w_recv, v_send, v_recv, p_send, p_recv,
@@ -111,19 +111,26 @@
         [weight_own[:, tail:].astype(F32), column], axis=1
     ).astype(BF16)
 
-    def take_plane(p):
-        plane_load(p).wait()
-        plane = vol[:, p].astype(F32).reshape(area, wide_in).astype(BF16)
-        plane = matmul(to_rows[...], plane).astype(BF16)
-        apart = matmul(plane, split[...])
+    def keep(apart, p, first_row, count):
         parts = [apart[:, :LANES], apart[:, LANES:]]
         parts.append(pltpu.roll(parts[1], 1, 1))
         for t in range(3):
             narrow = parts[t].astype(BF16)
-            for y in range(rows_in):
-                cells[t, p + 1, y + 1] = narrow[y * channels : (y + 1) * channels]
-
-    take_plane(planes_in - 1)
+            for y in range(count):
+                cells[t, p, first_row + y] = narrow[y * channels : (y + 1) * channels]
+
+    def take_plane(plane, p, count):
+        plane = plane.astype(F32).reshape(area, wide_in).astype(BF16)
+        plane = matmul(to_rows[...], plane).astype(BF16)
+        keep(matmul(plane, split[...]), p, 1, count)
+
+    ends = []
+    for p in range(planes_in):
+        plane_load(p).wait()
+        ends.append(vol[:, p].astype(F32)[:, rows_in - 1, :].astype(BF16))
+    ends = matmul(jnp.concatenate(ends, axis=0), split[...])
+    for p in range(planes_in):
+        keep(ends[p * channels : (p + 1) * channels], p + 1, rows_in, 1)
     pl.semaphore_wait(barrier, (n_col - 1) + (n_gz - 1) + 2)
 
     def send(src, dst, send_sem, recv_sem, there):
@@ -133,15 +140,13 @@
         )
 
     plane_copy = send(
-        cells.at[0:2, planes_in, 1 : rows_in + 1], cells.at[0:2, 0, 1 : rows_in + 1],
+        vol.at[:, planes_in - 1], edge,
         v_send.at[0], v_recv.at[0], (gz_next, col),
     )
     corner_copy = send(
         cells.at[0:2, planes_in, rows_in], cells.at[0:2, 0, 0],
         v_send.at[1], v_recv.at[1], (gz_next, col_next),
     )
-    plane_copy.start()
-    corner_copy.start()
     own_rows = pl.ds(pl.multiple_of(col * own, own), own)
     weight_copies = [
         send(
@@ -150,16 +155,18 @@
         )
         for d in range(1, n_col)
     ]
-    for copy in weight_copies:
-        copy.start()
-    full[own_rows] = weight[...]
-    for p in range(planes_in - 1):
-        take_plane(p)
     row_copy = send(
         cells.at[0:2, 1 : planes_in + 1, rows_in], cells.at[0:2, 1 : planes_in + 1, 0],
         v_send.at[2], v_recv.at[2], (gz, col_next),
     )
+    plane_copy.start()
     row_copy.start()
+    for copy in weight_copies:
+        copy.start()
+    corner_copy.start()
+    full[own_rows] = weight[...]
+    for p in range(planes_in):
+        take_plane(vol[:, p], p + 1, rows_in - 1)
 
     loads[2].wait()
     for g in range(outputs // group):
@@ -226,8 +233,8 @@
     plane_copy.wait()
     corner_copy.wait()
     row_copy.wait()
-    for y in range(rows_in + 1):
-        cells[2, 0, y] = turn(cells[1, 0, y], 1)
+    take_plane(edge[...], 0, rows_in)
+    cells[2, 0, 0] = turn(cells[1, 0, 0], 1)
     for p in range(1, planes_in + 1):
         cells[2, p, 0] = turn(cells[1, p, 0], 1)
     forward(border, reached)
@@ -262,13 +269,6 @@
         )
     for copy in term_copies:
         copy.start()
-
-    for copy in halo_copies:
-        copy.wait()
-    for j in range(rows + 1):
-        rolled[planes, j] = turn(deltas[planes, j], LANES - 1)
-    for k in range(planes):
-        rolled[k, rows] = turn(deltas[k, rows], LANES - 1)
 
     def backward(k):
         for sz in range(2):
@@ -302,7 +302,6 @@
             tall = matmul(from_rows[...], tall)
             igrad[:, 2 * k + pz] = tall.reshape(channels, rows_in, wide_in).astype(BF16)
 
-    backward(0)
 
     for copy in term_copies:
         copy.wait()
@@ -328,7 +327,15 @@
         return carry
 
     around(n_gz, piece_start, 0)
-    for k in range(1, planes - 1):
+    for copy in halo_copies:
+        copy.wait()
+    for j in range(rows + 1):
+        rolled[planes, j] = turn(deltas[planes, j], LANES - 1)
+    for k in range(planes):
+        rolled[k, rows] = turn(deltas[k, rows], LANES - 1)
+
+    half = planes // 2
+    for k in range(half):
         backward(k)
 
     def piece_sent(d, carry):
@@ -363,7 +370,8 @@
 
         around(n_gz, result_start, 0)
 
-    backward(planes - 1)
+    for k in range(half, planes):
+        backward(k)
 
     @pl.when(gz < owners)
     def _():
@@ -417,6 +425,7 @@
             pltpu.VMEM(weight.shape, BF16),
             pltpu.VMEM((1, own), BF16),
             pltpu.VMEM((own, taps_wide), BF16),
+            pltpu.VMEM((channels, rows_in, wide_in), BF16),
             pltpu.VMEM((3, planes_in + 1, rows_in + 1, channels, LANES), BF16),
             pltpu.VMEM((taps_wide, cells_out), BF16),
             pltpu.VMEM((outputs, taps_wide), BF16),
@@ -445,9 +454,9 @@
             dma((n_gz - 1,)), dma((owners,)),
         ],
         compiler_params=pltpu.CompilerParams(
-            collective_id=0, has_side_effects=True, vmem_limit_bytes=60 * 1024 * 1024
+            collective_id=0, has_side_effects=True, vmem_limit_bytes=40 * 1024 * 1024
         ),
-    )(volume, cotangent.reshape(outputs, blocks, wide), weight, bias[None, :])
+    )(pltpu.with_memory_space_constraint(volume, pltpu.HBM), *(pltpu.with_memory_space_constraint(x, pltpu.HBM) for x in (cotangent.reshape(outputs, blocks, wide), weight, bias[None, :])))
     return input_grad, filter_grad, bias_grad.reshape(own)
 
 

time: 31.7 us -> 29.4 us (0.927)
  local copies, waits for them, and re-layouts: 3.46 us -> 2.11 us
  Pallas kernels: 27.4 us -> 26.5 us
    unnamed x7 -> x3, local copies, waits for them, and re-layouts: 3.46 us -> 2.11 us
    pallas_call x1, Pallas kernels: 27.4 us -> 26.5 us  [local(): pl.pallas_call(functools.partial(kernel, n_gz, n_col, scale), out_shape=(...]
where the time goes in v3:
time: 29.4 us; the launch traced here: 29.2 us
  Pallas kernels  26.5 us (90%)
  local copies, waits for them, and re-layouts  2.11 us (7%)
  between operations  0.64 us (2%)
    pallas_call x1, Pallas kernels, local(): pl.pallas_call(functools.partial(kernel, n_gz, n_col, scale), out_shape=(...  26.5 us
    unnamed x3, local copies, waits for them, and re-layouts  2.11 us

profile of v3, /device:TPU:0, one launch (start us, length us, event | category | flops | bytes accessed | tf_op | source)
XLA Modules:
  0.0 29.2 jit_solution(15454705947735174680)
XLA Ops:
  0.6 26.5 %shard_map.67 = (bf16[32,8,8,256]{3,2,1,0:T(8,128)(2,1)S(1)}, f32[16,864]{1,0:T(8,128)S(1)}, f32[1,16]{1,0:T(1,128)S(1)}) custom-call(bf16[32,8,8,256]{3,2,1,0:T(8,128)(2,1)} %volume.1, bf16[64,16,128]{2,1,0:T(8,128)(2,1)} %bitcast.4, bf16[16,864]{1,0:T(8,128)(2,1)} %weight_in.1, bf16[1,16]{1,0:T(2,128)(2,1)} %bitcast.5), custom_call_target="tpu_custom_call" | custom-call | tf_op jit(solution)/shard_map/pallas_call | solution.py:413
  27.1 1.0 %copy.10 = bf16[32,8,8,256]{3,2,1,0:T(8,128)(2,1)} copy(bf16[32,8,8,256]{3,2,1,0:T(8,128)(2,1)S(1)} %get-tuple-element.12) | data formatting | bytes 2097152
  28.1 0.6 %copy.11 = f32[16,864]{1,0:T(8,128)} copy(f32[16,864]{1,0:T(8,128)S(1)} %get-tuple-element.13) | data formatting | bytes 110592
  28.7 0.5 %copy.12 = f32[16]{0:T(128)} copy(f32[16]{0:T(128)S(1)} %bitcast.3) | data formatting | bytes 128

commit v4 on v3

--- a/solution.py
+++ b/solution.py
@@ -224,19 +224,18 @@
             narrow = delta.astype(BF16)
             flat[:, start + place * LANES : start + (place + 1) * LANES] = narrow
             deltas[k, j] = narrow
-            rolled[k, j] = turn(narrow, LANES - 1)
         return stop
 
     inside = [(k, j) for k in range(1, planes) for j in range(1, rows)]
     border = [(0, j) for j in range(rows)] + [(k, 0) for k in range(1, planes)]
     reached = forward(inside, 0)
+    row_copy.wait()
+    for p in range(1, planes_in + 1):
+        cells[2, p, 0] = turn(cells[1, p, 0], 1)
     plane_copy.wait()
     corner_copy.wait()
-    row_copy.wait()
     take_plane(edge[...], 0, rows_in)
     cells[2, 0, 0] = turn(cells[1, 0, 0], 1)
-    for p in range(1, planes_in + 1):
-        cells[2, p, 0] = turn(cells[1, p, 0], 1)
     forward(border, reached)
     halo_copies = [
         send(
@@ -269,6 +268,9 @@
         )
     for copy in term_copies:
         copy.start()
+    for k in range(planes):
+        for j in range(rows):
+            rolled[k, j] = turn(deltas[k, j], LANES - 1)
 
     def backward(k):
         for sz in range(2):

time: 29.4 us -> 29.3 us (level)
  no operation moved by 1% of the time
where the time goes in v4:
time: 29.3 us; the launch traced here: 29.1 us
  Pallas kernels  26.4 us (90%)
  local copies, waits for them, and re-layouts  2.11 us (7%)
  between operations  0.64 us (2%)
    pallas_call x1, Pallas kernels, local(): pl.pallas_call(functools.partial(kernel, n_gz, n_col, scale), out_shape=(...  26.4 us
    unnamed x3, local copies, waits for them, and re-layouts  2.11 us

profile of v4, /device:TPU:0, one launch (start us, length us, event | category | flops | bytes accessed | tf_op | source)
XLA Modules:
  0.0 29.1 jit_solution(9484586351426870820)
XLA Ops:
  0.6 26.4 %shard_map.67 = (bf16[32,8,8,256]{3,2,1,0:T(8,128)(2,1)S(1)}, f32[16,864]{1,0:T(8,128)S(1)}, f32[1,16]{1,0:T(1,128)S(1)}) custom-call(bf16[32,8,8,256]{3,2,1,0:T(8,128)(2,1)} %volume.1, bf16[64,16,128]{2,1,0:T(8,128)(2,1)} %bitcast.4, bf16[16,864]{1,0:T(8,128)(2,1)} %weight_in.1, bf16[1,16]{1,0:T(2,128)(2,1)} %bitcast.5), custom_call_target="tpu_custom_call" | custom-call | tf_op jit(solution)/shard_map/pallas_call | solution.py:415
  27.0 1.0 %copy.10 = bf16[32,8,8,256]{3,2,1,0:T(8,128)(2,1)} copy(bf16[32,8,8,256]{3,2,1,0:T(8,128)(2,1)S(1)} %get-tuple-element.12) | data formatting | bytes 2097152
  28.0 0.6 %copy.11 = f32[16,864]{1,0:T(8,128)} copy(f32[16,864]{1,0:T(8,128)S(1)} %get-tuple-element.13) | data formatting | bytes 110592
  28.6 0.5 %copy.12 = f32[16]{0:T(128)} copy(f32[16]{0:T(128)S(1)} %bitcast.3) | data formatting | bytes 128
